TPU v7x, 32 devices: a whole 2x2x4 slice. The times are simulated.
32 devices in a mesh: dp: 4 (over z), sq: 8 (over y, x, core).
Axes of the slice: x: 2, y: 2, z: 4, core: 2. Of those that a mesh axis runs over, the one named last changes fastest.
Arguments:
- frames: bfloat16 [4, 1024, 1024], P('dp', 'sq'), may hold values from -6 to 6
- norm1_gain: float32 [1024], replicated, may hold values from 0.5 to 1.5
- w_qkv: bfloat16 [1024, 3072], replicated, may hold values from -0.1875 to 0.1875
- w_out: bfloat16 [1024, 1024], replicated, may hold values from -0.75 to 0.75
- norm2_gain: float32 [1024], replicated, may hold values from 0.5 to 1.5
- w_up: bfloat16 [1024, 4096], replicated, may hold values from -0.1875 to 0.1875
- w_down: bfloat16 [4096, 1024], replicated, may hold values from -0.09375 to 0.09375
- lengths: int32 [4, 8], P('dp'), may hold values from 1 to 896, as said below
- cotangent: bfloat16 [4, 1024, 1024], P('dp', 'sq'), may hold values from -6 to 6
Outputs:
- out: bfloat16 [4, 1024, 1024], P('dp', 'sq')
- d_in: float32 [4, 1024, 1024], P('dp', 'sq')
- g_norm1: float32 [1024], P('sq')
- g_qkv: float32 [1024, 3072], P('sq')
- g_out: float32 [1024, 1024], P('sq')
- g_norm2: float32 [1024], P('sq')
- g_up: float32 [1024, 4096], P('sq')
- g_down: float32 [4096, 1024], P('sq')
Inputs may be any that keep to these rules, and one draw needn't show every extreme that they name: Each row's lengths sum to 1024. In each row exactly one item has 896 frames and is neither the first nor the last item of the row; the other items share the remaining 128 frames.
All inputs are finite; a program needn't handle non-finite values.
Results may differ from a plain program's by a relative error of at most 0.025.
Values may be sent and summed in bfloat16 or wider, within the bound.
A program may use at most 256 MiB of HBM per device.

v0:
```python
import jax
import jax.numpy as jnp
from jax import lax
from jax.sharding import PartitionSpec as P

HEADS = 16
HEAD_DIM = 64
EPSILON = 1e-05
NEG_FILL = -1000000000.0
START_MAX = -1e30


def norm_scaled(values, gain):
    return values * lax.rsqrt(jnp.mean(values * values, axis=-1, keepdims=True) + EPSILON) * gain


def segment_ids(positions, item_ends):
    return jnp.sum((positions[None, :, None] >= item_ends[:, None, :]).astype(jnp.int32), axis=2)


def visible(query_pos, query_seg, key_pos, key_seg):
    return (key_pos[None, None, :] <= query_pos[None, :, None]) & (
        key_seg[:, None, :] == query_seg[:, :, None]
    )


def block_size(count, limit):
    for candidate in range(min(count, limit), 0, -1):
        if count % candidate == 0:
            return candidate
    return count


def over_blocks(carry, arrays, start, step_fn, limit):
    count = arrays[0].shape[1]
    size = block_size(count, limit)
    number = count // size
    if number == 1:
        return step_fn(carry, arrays, start)
    stacked = tuple(
        (
            jnp.swapaxes(member.reshape((member.shape[0], number, size) + member.shape[2:]), 0, 1)
            for member in arrays
        )
    )

    def turn(state, item):
        offset, pieces = item
        return (step_fn(state, pieces, start + offset * size), None)

    offsets = jnp.arange(number, dtype=jnp.int32)
    return lax.scan(turn, carry, (offsets, stacked))[0]


def contract_rows(left, right):
    return lax.dot_general(
        left, right, (((0,), (0,)), ((), ())), preferred_element_type=jnp.float32
    )


def times_transpose(left, right):
    return lax.dot_general(
        left, right, (((1,), (1,)), ((), ())), preferred_element_type=jnp.float32
    )


def heads_flat(values, batch, rows, width):
    return values.transpose(0, 2, 1, 3).reshape(batch * rows, width)


def shards(frames, norm1_gain, w_qkv, w_out, norm2_gain, w_up, w_down, lengths, cotangent):
    batch = frames.shape[0]
    rows = frames.shape[1]
    width = frames.shape[2]
    factor = HEAD_DIM ** (-0.5)
    first = lax.axis_index("sq") * rows
    query_pos = first + jnp.arange(rows, dtype=jnp.int32)
    item_ends = jnp.cumsum(lengths, axis=1)
    query_seg = segment_ids(query_pos, item_ends)
    frames_own = frames.reshape(batch * rows, width).astype(jnp.float32)
    hidden1, norm1_pull = jax.vjp(norm_scaled, frames_own, norm1_gain)
    hidden1_low = hidden1.astype(jnp.bfloat16)
    mixed = jnp.dot(hidden1_low, w_qkv, preferred_element_type=jnp.float32).astype(jnp.bfloat16)
    query_rows = mixed[:, :width].reshape(batch, rows, width)
    key_rows = mixed[:, width : 2 * width].reshape(batch, rows, width)
    value_rows = mixed[:, 2 * width :].reshape(batch, rows, width)
    queries = query_rows.reshape(batch, rows, HEADS, HEAD_DIM)
    keys_own = key_rows.reshape(batch, rows, HEADS, HEAD_DIM)
    values_own = value_rows.reshape(batch, rows, HEADS, HEAD_DIM)

    def forward_step(carry, pieces, start):
        key_piece, value_piece = pieces
        count = key_piece.shape[1]
        key_pos = start + jnp.arange(count, dtype=jnp.int32)
        key_seg = segment_ids(key_pos, item_ends)

        def forward_work(state):
            running_max, running_sum, accum = state
            keys_block = key_piece.reshape(batch, count, HEADS, HEAD_DIM)
            values_block = value_piece.reshape(batch, count, HEADS, HEAD_DIM)
            scores = (
                jnp.einsum(
                    "rqhd,rkhd->rhqk", queries, keys_block, preferred_element_type=jnp.float32
                )
                * factor
            )
            mask = visible(query_pos, query_seg, key_pos, key_seg)[:, None]
            scores = jnp.where(mask, scores, NEG_FILL)
            new_max = jnp.maximum(running_max, jnp.max(scores, axis=-1))
            weights = jnp.where(mask, jnp.exp(scores - new_max[..., None]), 0.0)
            decay = jnp.exp(running_max - new_max)
            new_sum = decay * running_sum + jnp.sum(weights, axis=-1)
            update = jnp.einsum(
                "rhqk,rkhd->rhqd",
                weights.astype(jnp.bfloat16),
                values_block,
                preferred_element_type=jnp.float32,
            )
            return (new_max, new_sum, decay[..., None] * accum + update)

        return lax.cond(start <= query_pos[-1], forward_work, lambda state: state, carry)

    start_state = (
        jnp.full((batch, HEADS, rows), START_MAX, jnp.float32),
        jnp.zeros((batch, HEADS, rows), jnp.float32),
        jnp.zeros((batch, HEADS, rows, HEAD_DIM), jnp.float32),
    )
    final_max, final_sum, accum = over_blocks(
        start_state,
        (
            lax.all_gather(key_rows, "sq", axis=1, tiled=True),
            lax.all_gather(value_rows, "sq", axis=1, tiled=True),
        ),
        jnp.int32(0),
        forward_step,
        512,
    )
    attended = heads_flat(accum / final_sum[..., None], batch, rows, width)
    log_total = final_max + jnp.log(final_sum)
    attended_low = attended.astype(jnp.bfloat16)
    middle = frames_own + jnp.dot(attended_low, w_out, preferred_element_type=jnp.float32)
    hidden2, norm2_pull = jax.vjp(norm_scaled, middle, norm2_gain)
    hidden2_low = hidden2.astype(jnp.bfloat16)
    upward = jnp.dot(hidden2_low, w_up, preferred_element_type=jnp.float32)
    active, gelu_pull = jax.vjp(jax.nn.gelu, upward)
    active_low = active.astype(jnp.bfloat16)
    result = middle + jnp.dot(active_low, w_down, preferred_element_type=jnp.float32)
    grad_top = cotangent.reshape(batch * rows, width).astype(jnp.float32)
    grad_branch = grad_top.astype(jnp.bfloat16)
    grad_down = contract_rows(active_low, grad_branch)
    grad_active = times_transpose(grad_branch, w_down)
    grad_upward = gelu_pull(grad_active)[0].astype(jnp.bfloat16)
    grad_up = contract_rows(hidden2_low, grad_upward)
    grad_hidden2 = times_transpose(grad_upward, w_up)
    grad_middle_part, grad_gain2 = norm2_pull(grad_hidden2)
    grad_middle = grad_top + grad_middle_part
    grad_attn = grad_middle.astype(jnp.bfloat16)
    grad_outproj = contract_rows(attended_low, grad_attn)
    grad_attended = times_transpose(grad_attn, w_out).astype(jnp.bfloat16)
    grad_rows_own = grad_attended.reshape(batch, rows, width)
    grad_heads = grad_attended.reshape(batch, rows, HEADS, HEAD_DIM)
    delta_rows = jnp.sum(
        (grad_attended.astype(jnp.float32) * attended).reshape(batch, rows, HEADS, HEAD_DIM), axis=3
    )
    delta = delta_rows.transpose(0, 2, 1)

    def query_step(carry, pieces, start):
        key_piece, value_piece = pieces
        count = key_piece.shape[1]
        key_pos = start + jnp.arange(count, dtype=jnp.int32)
        key_seg = segment_ids(key_pos, item_ends)

        def query_work(grad_query):
            keys_block = key_piece.reshape(batch, count, HEADS, HEAD_DIM)
            values_block = value_piece.reshape(batch, count, HEADS, HEAD_DIM)
            scores = (
                jnp.einsum(
                    "rqhd,rkhd->rhqk", queries, keys_block, preferred_element_type=jnp.float32
                )
                * factor
            )
            mask = visible(query_pos, query_seg, key_pos, key_seg)[:, None]
            shares = jnp.where(mask, jnp.exp(scores - log_total[..., None]), 0.0)
            grad_shares = jnp.einsum(
                "rqhd,rkhd->rhqk", grad_heads, values_block, preferred_element_type=jnp.float32
            )
            grad_scores = (shares * (grad_shares - delta[..., None])).astype(jnp.bfloat16)
            return grad_query + jnp.einsum(
                "rhqk,rkhd->rhqd", grad_scores, keys_block, preferred_element_type=jnp.float32
            )

        return lax.cond(start <= query_pos[-1], query_work, lambda state: state, carry)

    zero_query = jnp.zeros((batch, HEADS, rows, HEAD_DIM), jnp.float32)
    grad_query = over_blocks(
        zero_query,
        (
            lax.all_gather(key_rows, "sq", axis=1, tiled=True),
            lax.all_gather(value_rows, "sq", axis=1, tiled=True),
        ),
        jnp.int32(0),
        query_step,
        512,
    )

    def key_step(carry, pieces, start):
        query_piece, grad_piece, total_piece, delta_piece = pieces
        count = query_piece.shape[1]
        remote_pos = start + jnp.arange(count, dtype=jnp.int32)
        remote_seg = segment_ids(remote_pos, item_ends)

        def key_work(state):
            grad_key, grad_value = state
            remote_queries = query_piece.reshape(batch, count, HEADS, HEAD_DIM)
            remote_grads = grad_piece.reshape(batch, count, HEADS, HEAD_DIM)
            scores = (
                jnp.einsum(
                    "rqhd,rkhd->rhqk", remote_queries, keys_own, preferred_element_type=jnp.float32
                )
                * factor
            )
            mask = visible(remote_pos, remote_seg, query_pos, query_seg)[:, None]
            shares = jnp.where(
                mask, jnp.exp(scores - total_piece.transpose(0, 2, 1)[..., None]), 0.0
            )
            grad_value = grad_value + jnp.einsum(
                "rhqk,rqhd->rhkd",
                shares.astype(jnp.bfloat16),
                remote_grads,
                preferred_element_type=jnp.float32,
            )
            grad_shares = jnp.einsum(
                "rqhd,rkhd->rhqk", remote_grads, values_own, preferred_element_type=jnp.float32
            )
            grad_scores = (
                shares * (grad_shares - delta_piece.transpose(0, 2, 1)[..., None])
            ).astype(jnp.bfloat16)
            grad_key = grad_key + jnp.einsum(
                "rhqk,rqhd->rhkd", grad_scores, remote_queries, preferred_element_type=jnp.float32
            )
            return (grad_key, grad_value)

        return lax.cond(start + count - 1 >= first, key_work, lambda state: state, carry)

    grad_key, grad_value = over_blocks(
        (zero_query, zero_query),
        (
            lax.all_gather(query_rows, "sq", axis=1, tiled=True),
            lax.all_gather(grad_rows_own, "sq", axis=1, tiled=True),
            lax.all_gather(
                log_total.transpose(0, 2, 1).astype(jnp.bfloat16), "sq", axis=1, tiled=True
            ).astype(jnp.float32),
            lax.all_gather(delta_rows.astype(jnp.bfloat16), "sq", axis=1, tiled=True).astype(
                jnp.float32
            ),
        ),
        jnp.int32(0),
        key_step,
        512,
    )
    grad_mixed = jnp.concatenate(
        [
            heads_flat(grad_query * factor, batch, rows, width),
            heads_flat(grad_key * factor, batch, rows, width),
            heads_flat(grad_value, batch, rows, width),
        ],
        axis=1,
    ).astype(jnp.bfloat16)
    grad_qkv = contract_rows(hidden1_low, grad_mixed)
    grad_hidden1 = times_transpose(grad_mixed, w_qkv)
    grad_frames_part, grad_gain1 = norm1_pull(grad_hidden1)
    grad_frames = (grad_middle + grad_frames_part).reshape(batch, rows, width)
    result_rows = result.astype(jnp.bfloat16).reshape(batch, rows, width)
    shares_sq = (
        lax.psum_scatter(grad_gain1, "sq", scatter_dimension=0, tiled=True),
        lax.psum_scatter(grad_qkv, "sq", scatter_dimension=0, tiled=True),
        lax.psum_scatter(grad_outproj, "sq", scatter_dimension=0, tiled=True),
        lax.psum_scatter(grad_gain2, "sq", scatter_dimension=0, tiled=True),
        lax.psum_scatter(grad_up, "sq", scatter_dimension=0, tiled=True),
        lax.psum_scatter(grad_down, "sq", scatter_dimension=0, tiled=True),
    )
    totals = (
        lax.psum(shares_sq[0].astype(jnp.bfloat16), "dp").astype(jnp.float32),
        lax.psum(shares_sq[1].astype(jnp.bfloat16), "dp").astype(jnp.float32),
        lax.psum(shares_sq[2].astype(jnp.bfloat16), "dp").astype(jnp.float32),
        lax.psum(shares_sq[3].astype(jnp.bfloat16), "dp").astype(jnp.float32),
        lax.psum(shares_sq[4].astype(jnp.bfloat16), "dp").astype(jnp.float32),
        lax.psum(shares_sq[5].astype(jnp.bfloat16), "dp").astype(jnp.float32),
    )
    return (
        result_rows,
        grad_frames,
        totals[0],
        totals[1],
        totals[2],
        totals[3],
        totals[4],
        totals[5],
    )


def solution(mesh):
    return jax.shard_map(
        shards,
        mesh=mesh,
        in_specs=(
            P("dp", "sq", None),
            P(),
            P(),
            P(),
            P(),
            P(),
            P(),
            P("dp", None),
            P("dp", "sq", None),
        ),
        out_specs=(
            P("dp", "sq", None),
            P("dp", "sq", None),
            P("sq"),
            P("sq", None),
            P("sq", None),
            P("sq"),
            P("sq", None),
            P("sq", None),
        ),
        check_vma=False,
    )
```

profile of v0, /device:TPU:0, one launch (start us, length us, event | category | flops | bytes accessed | tf_op | source)
XLA Modules:
  0.0 698.9 jit_solution(101815978232163255)
XLA Ops:
  9.0 4.0 convolution_convert_fusion
  18.7 26.0 %all-gather.9.cloned.1.call-done = bf16[1024,1024]{1,0:T(8,128)(2,1)} async-done(((bf16[128,1024]{1,0:T(8,128)(2,1)}), bf16[1024,1024]{1,0:T(8,128)(2,1)}) %all-gather.9.cloned.1.call-update) | async-done | bytes 2097168 | tf_op jit(solution)/shard_map/all_gather | solution.py:131
  48.6 26.5 %all-gather.11.cloned.1.call-done = bf16[1024,1024]{1,0:T(8,128)(2,1)} async-done(((bf16[128,1024]{1,0:T(8,128)(2,1)}), bf16[1024,1024]{1,0:T(8,128)(2,1)}) %all-gather.11.cloned.1.call-update) | async-done | bytes 2097168 | tf_op jit(solution)/shard_map/all_gather | solution.py:132
  79.1 13.9 %while.45 = (s32[]{:T(128)}, f32[1,16,128]{2,1,0:T(8,128)S(1)}, f32[1,16,128]{2,1,0:T(8,128)S(1)}, f32[1,16,128,64]{2,3,1,0:T(8,128)S(1)}, s32[2]{0:T(128)S(1)},...) while((s32[]{:T(128)}, f32[1,16,128]{2,1,0:T(8,128)S(1)}, ...), condition=%wide.region_9.10_spmd, body=%wide.region_3.9_spmd.sunk | while | flops 282544640 | bytes 20628860 | solution.py:52
  83.0 6.1 conditional.8
  98.3 4.9 fusion.92
  103.2 7.7 %fusion.60 = bf16[128,4096]{1,0:T(8,128)(2,1)S(1)} fusion(f32[128,4096]{1,0:T(8,128)S(1)} %fusion.92, bf16[4096,1024]{1,0:T(8,128)(2,1)} %param.27, bf16[1,128,1024]{2,1,0:T(8,128)(2,1)S(1)} %copy-done.18), kind=kOutput, calls=%fused_computation.80 | convolution fusion | flops 1084227584 | bytes 11796480 | tf_op jit(solution)/shard_map/dot_general | solution.py:62
  124.1 4.0 copy.73
  129.7 15.0 %all_gather.25 = bf16[1,1024,16]{1,2,0:T(8,128)(2,1)S(1)} all-gather(bf16[1,128,16]{1,2,0:T(8,128)(2,1)S(1)} %bitcast_convert_fusion), channel_id=1, replica_groups=mesh['dp'=4,'sq'=8] {'sq'}, dimensions={1}, use_global_device_ids=true | all-gather | bytes 36864 | tf_op jit(solution)/shard_map/all_gather | solution.py:253
  145.3 8.0 %all_gather.23 = bf16[1,1024,16]{1,2,0:T(8,128)(2,1)S(1)} all-gather(bf16[1,128,16]{1,2,0:T(8,128)(2,1)S(1)} %get-tuple-element.1073), channel_id=1, replica_groups=mesh['dp'=4,'sq'=8] {'sq'}, dimensions={1}, use_global_device_ids=true | all-gather | bytes 36864 | tf_op jit(solution)/shard_map/all_gather | solution.py:250
  155.3 20.4 %while.46 = (s32[]{:T(128)}, f32[1,16,128,64]{2,3,1,0:T(8,128)}, s32[2]{0:T(128)}, s32[128]{0:T(128)}, s32[1,8]{1,0:T(1,128)}, /*index=5*/s32[1,128]{1,0:T(1,128...) while((s32[]{:T(128)}, f32[1,16,128,64]{2,3,1,0:T(8,128)}, ...), condition=%wide.region_17.18_spmd, body=%wide.region_13.17_spmd.sunk | while | flops 409285120 | bytes 17499484 | solution.py:52
  159.7 11.6 %conditional.9 = (f32[1,16,128,64]{2,3,1,0:T(8,128)}) conditional(s32[]{:T(128)} %convert_element_type.291, f32[1,16,128,64]{2,3,1,0:T(8,128)} %get-tuple-element.1437, (s32[]{:T(128)}, s32[512]{0:T(512)S(1)}, s32[128]{0:T(128)}, s32[1,512,8]{1,2,0:T(8,128)S(1)}, s32[1,128]{1,0:T(1,128)}, /*index=5*/bf16[2,1,512,1024]{2,3,1,0:T(8,128)(2,1)}, ...), branch_computations={%region_14.14_spmd, %region_15.16_spmd} | conditional | flops 409276416 | bytes 17476628 | solution.py:192
  165.8 5.5 fusion.23
  177.5 4.0 copy.75
  182.4 36.2 %while.47 = (s32[]{:T(128)}, f32[1,16,128,64]{2,3,1,0:T(8,128)S(1)}, f32[1,16,128,64]{2,3,1,0:T(8,128)}, s32[2]{0:T(128)S(1)}, s32[]{:T(128)}, /*index=5*/s32[1,...) while((s32[]{:T(128)}, ...), condition=%wide.region_22.23_spmd.clone.clone, body=%wide.region_18.22_spmd.clone.clone.sunk | while | flops 547828352 | bytes 28265440 | solution.py:52
  184.5 16.3 %conditional.10 = ((f32[1,16,128,64]{2,3,1,0:T(8,128)S(1)}, f32[1,16,128,64]{2,3,1,0:T(8,128)})) conditional(s32[]{:T(128)} %convert_element_type.293, (f32[1,16,128,64]{2,3,1,0:T(8,128)S(1)}, f32[1,16,128,64]{2,3,1,0:T(8,128)}) %tuple.150, (s32[]{:T(128)}, s32[]{:T(128)}, s32[512]{0:T(512)S(1)}, s32[1,128]{1,0:T(1,128)S(1)}, ...), branch_computations={%region_19.19_spmd, %region_20.21_spmd} | conditional | flops 547819648 | bytes 28242020 | solution.py:243
  190.0 6.2 fusion.42
  196.2 4.5 fusion.43
  202.8 15.9 %conditional.10 = ((f32[1,16,128,64]{2,3,1,0:T(8,128)S(1)}, f32[1,16,128,64]{2,3,1,0:T(8,128)})) conditional(s32[]{:T(128)} %convert_element_type.293, (f32[1,16,128,64]{2,3,1,0:T(8,128)S(1)}, f32[1,16,128,64]{2,3,1,0:T(8,128)}) %tuple.150, (s32[]{:T(128)}, s32[]{:T(128)}, s32[512]{0:T(512)S(1)}, s32[1,128]{1,0:T(1,128)S(1)}, ...), branch_computations={%region_19.19_spmd, %region_20.21_spmd} | conditional | flops 547819648 | bytes 28242020 | solution.py:243
  208.3 6.2 fusion.42
  214.4 4.2 fusion.43
  219.8 7.5 %fusion.72 = f32[1024,3072]{1,0:T(8,128)} fusion(bf16[128,1024]{0,1:T(8,128)(2,1)S(1)} %bitcast.228, bf16[128,1024]{0,1:T(8,128)(2,1)S(1)} %bitcast.230, bf16[128,1024]{0,1:T(8,128)(2,1)} %bitcast.226, bf16[1,128,1024]{2,1,0:T(8,128)(2,1)S(1)} %copy-done.4, f32[1024]{0:T(1024)S(1)} %copy-done.30, f32[128]{0:T(128)S(1)} %copy-done.38), kind=kOutput, calls=%fused_computation.111 | convolution fusion | flops 808189952 | bytes 13636096 | tf_op jit(solution)/shard_map/dot_general | solution.py:56
  228.5 11.2 %fusion.91 = f32[1024,4096]{1,0:T(8,128)} fusion(bf16[128,4096]{1,0:T(8,128)(2,1)S(1)} %copy-done.9, f32[128,1024]{1,0:T(8,128)S(1)} %get-tuple-element.1089, f32[1024]{0:T(1024)S(1)} %copy-done.29, f32[128]{0:T(128)S(1)} %copy-done.35), kind=kOutput, calls=%fused_computation.140 | convolution fusion | flops 1074135040 | bytes 18354688 | tf_op jit(solution)/shard_map/dot_general | solution.py:56
  241.9 8.9 %fusion.74 = f32[4096,1024]{1,0:T(8,128)} fusion(bf16[1,128,1024]{2,1,0:T(8,128)(2,1)S(1)} %copy-done.19, f32[128,4096]{1,0:T(8,128)S(1)} %copy-done.3), kind=kOutput, calls=%fused_computation.113 | convolution fusion | flops 1078460416 | bytes 19136512 | tf_op jit(solution)/shard_map/dot_general | solution.py:56
  252.8 67.5 %reduce-scatter.5.cloned.1.call-done = f32[128,3072]{1,0:T(8,128)} async-done(((f32[1024,3072]{1,0:T(8,128)}), f32[128,3072]{1,0:T(8,128)}) %reduce-scatter.5.cloned.1.call-update) | async-done | bytes 1572880 | tf_op jit(solution)/shard_map/reduce_scatter | solution.py:276
  322.6 117.6 %reduce-scatter.9.cloned.1.call-done = f32[128,4096]{1,0:T(8,128)} async-done(((f32[1024,4096]{1,0:T(8,128)}), f32[128,4096]{1,0:T(8,128)}) %reduce-scatter.9.cloned.1.call-update) | async-done | bytes 2097168 | tf_op jit(solution)/shard_map/reduce_scatter | solution.py:279
  442.9 117.3 %reduce-scatter.11.cloned.1.call-done = f32[512,1024]{1,0:T(8,128)} async-done(((f32[4096,1024]{1,0:T(8,128)}), f32[512,1024]{1,0:T(8,128)}) %reduce-scatter.11.cloned.1.call-update) | async-done | bytes 2097168 | tf_op jit(solution)/shard_map/reduce_scatter | solution.py:280
  564.8 5.7 fusion.62
  570.6 5.2 fusion.66
  575.8 13.8 %all-reduce.2 = (bf16[1024]{0:T(1024)(128)(2,1)S(1)}, bf16[1024]{0:T(1024)(128)(2,1)S(1)}) all-reduce(f32[1024]{0:T(1024)S(1)} %get-tuple-element.989, f32[1024]{0:T(1024)S(1)} %copy-done.36), channel_id=6, replica_groups=mesh['dp'=4,'sq'=8] {'sq'}, use_global_device_ids=true, to_apply=%region_25.26.clone | all-reduce | flops 2048 | bytes 12288
  589.8 12.4 %all-reduce.3 = (bf16[128]{0:T(256)(128)(2,1)S(1)}, bf16[128]{0:T(256)(128)(2,1)S(1)}) all-reduce(bf16[128]{0:T(256)(128)(2,1)S(1)} %dynamic-slice.7, bf16[128]{0:T(256)(128)(2,1)S(1)} %dynamic-slice.6), channel_id=1, replica_groups=mesh['dp'=4,'sq'=8] {'dp'}, use_global_device_ids=true, to_apply=%region_26.27 | all-reduce | flops 256 | bytes 1024 | tf_op jit(solution)/shard_map/psum | solution.py:283
  604.2 81.7 %all-reduce.7.cloned.1.call-done = (bf16[128,3072]{1,0:T(8,128)(2,1)}, bf16[128,1024]{1,0:T(8,128)(2,1)}, bf16[128,4096]{1,0:T(8,128)(2,1)}, bf16[512,1024]{1,0:T(8,128)(2,1)}) async-done(((bf16[128,3072]{1,0:T(8,128)(2,1)}, bf16[128,1024]{1,0:T(8,128)(2,1)}, bf16[128,4096]{1,0:T(8,128)(2,1)}, bf16[512,1024]{1,0:T(8,128)(2,1)}), (bf16[128,3072]{1,0:T(8,128)(2,1)}, bf16[128,1024]{1,0:T(8,128)(2,1)}, ...) | async-done | bytes 3145744 | tf_op jit(solution)/shard_map/psum | solution.py:284
  (234 shorter events, 101.9 us)
Async XLA Ops:
  7.2 89.5 %copy-start = (bf16[1024,1024]{1,0:T(8,128)(2,1)S(1)}, bf16[1024,1024]{1,0:T(8,128)(2,1)}, u32[]{:S(2)}) copy-start(bf16[1024,1024]{1,0:T(8,128)(2,1)} %param.24) | copy-start | bytes 6291460
  7.2 37.5 %all-gather.9.cloned.1.call-start = ((), (), s32[]{:S(2)}) async-start(), calls=%async_computation.8 | async-start | bytes 2359296 | tf_op jit(solution)/shard_map/all_gather | solution.py:131
  13.0 4.1 copy-start.42
  14.0 61.1 %all-gather.11.cloned.1.call-start = ((), (), s32[]{:S(2)}) async-start(), calls=%async_computation.9 | async-start | bytes 2359296 | tf_op jit(solution)/shard_map/all_gather | solution.py:132
  14.7 109.4 %all-gather.13.cloned.1.call-start = ((), (), s32[]{:S(2)}) async-start(), calls=%async_computation.10 | async-start | bytes 2359296 | tf_op jit(solution)/shard_map/all_gather | solution.py:248
  15.4 162.1 %all-gather.15.cloned.1.call-start = ((), (), s32[]{:S(2)}) async-start(), calls=%async_computation.11 | async-start | bytes 2359296 | tf_op jit(solution)/shard_map/all_gather | solution.py:249
  92.9 5.3 copy-start.32
  98.2 16.3 %copy-start.34 = (f32[128]{0:T(128)}, f32[128]{0:T(128)S(1)}, u32[]{:S(2)}) copy-start(f32[128]{0:T(128)S(1)} %fusion.88) | copy-start | bytes 1540
  98.3 4.9 copy-start.18
  98.3 12.7 %slice-start = ((s8[8388608]{0:T(1024)(128)(4,1)}), s8[4194304]{0:T(1024)(128)(4,1)S(1)}, s32[]{:S(2)}) async-start(s8[8388608]{0:T(1024)(128)(4,1)} %bitcast.209), calls=%async_computation.13 | async-start | bytes 8388608
  103.2 7.8 %copy-start.2 = (f32[128,4096]{1,0:T(8,128)}, f32[128,4096]{1,0:T(8,128)S(1)}, u32[]{:S(2)}) copy-start(f32[128,4096]{1,0:T(8,128)S(1)} %fusion.92) | copy-start | bytes 6291460
  103.2 7.8 %slice-start.1 = ((s8[8388608]{0:T(1024)(128)(4,1)}), s8[4194304]{0:T(1024)(128)(4,1)S(1)}, s32[]{:S(2)}) async-start(s8[8388608]{0:T(1024)(128)(4,1)} %bitcast.209), calls=%async_computation.14 | async-start | bytes 8388608
  117.3 133.6 %reduce-scatter.7.cloned.1.call-start = ((), (), s32[]{:S(2)}) async-start(), calls=%async_computation.5 | async-start | bytes 4718592 | tf_op jit(solution)/shard_map/reduce_scatter | solution.py:277
  121.3 198.9 %reduce-scatter.5.cloned.1.call-start = ((), (), s32[]{:S(2)}) async-start(), calls=%async_computation.4 | async-start | bytes 14155776 | tf_op jit(solution)/shard_map/reduce_scatter | solution.py:276
  177.5 4.9 copy-start.27
  177.5 4.9 copy-start.33
  182.4 37.4 %copy-start.30 = (f32[1024]{0:T(1024)S(1)}, f32[1024]{0:T(1024)}, u32[]{:S(2)}) copy-start(f32[1024]{0:T(1024)} %param.22) | copy-start | bytes 12292
  182.4 37.4 %copy-start.38 = (f32[128]{0:T(128)S(1)}, f32[128]{0:T(128)}, u32[]{:S(2)}) copy-start(f32[128]{0:T(128)} %copy-done.37) | copy-start | bytes 1540
  196.2 4.5 copy-start.16
  214.4 4.2 copy-start.16
  219.7 7.6 %copy-start.23 = (bf16[1,16,128,64]{2,3,1,0:T(8,128)(2,1)}, bf16[1,16,128,64]{2,3,1,0:T(8,128)(2,1)S(1)}, u32[]{:S(2)}) copy-start(bf16[1,16,128,64]{2,3,1,0:T(8,128)(2,1)S(1)} %convert.20) | copy-start | bytes 786436
  219.8 7.5 %copy-start.25 = (bf16[1,16,128,64]{2,3,1,0:T(8,128)(2,1)}, bf16[1,16,128,64]{2,3,1,0:T(8,128)(2,1)S(1)}, u32[]{:S(2)}) copy-start(bf16[1,16,128,64]{2,3,1,0:T(8,128)(2,1)S(1)} %multiply_convert_fusion.2) | copy-start | bytes 786436
  227.3 212.8 %reduce-scatter.9.cloned.1.call-start = ((), (), s32[]{:S(2)}) async-start(), calls=%async_computation.6 | async-start | bytes 18874368 | tf_op jit(solution)/shard_map/reduce_scatter | solution.py:279
  239.7 320.4 %reduce-scatter.11.cloned.1.call-start = ((), (), s32[]{:S(2)}) async-start(), calls=%async_computation.7 | async-start | bytes 18874368 | tf_op jit(solution)/shard_map/reduce_scatter | solution.py:280
  250.9 435.0 %all-reduce.7.cloned.1.call-start = ((), (), s32[]{:S(2)}) async-start(), calls=%async_computation.12 | async-start | bytes 6291456 | tf_op jit(solution)/shard_map/psum | solution.py:284
  564.8 5.8 copy-start.22
  564.8 5.8 copy-start.24
  564.8 5.8 copy-start.26
  564.8 5.8 copy-start.39
  570.6 5.2 copy-start.36
  570.6 32.6 %copy-start.41 = (f32[128]{0:T(128)S(1)}, f32[128]{0:T(128)}, u32[]{:S(2)}) copy-start(f32[128]{0:T(128)} %copy-done.40) | copy-start | bytes 1540
  570.6 32.6 %copy-start.6 = (f32[128,1024]{1,0:T(8,128)S(1)}, f32[128,1024]{1,0:T(8,128)}, u32[]{:S(2)}) copy-start(f32[128,1024]{1,0:T(8,128)} %copy-done.5) | copy-start | bytes 1572868
  (25 other events, 47.7 us)
Sparse Core Ops, SparseCore 0:
  14.1 30.5 all-gather.8
  47.2 27.8 all-gather.10
  77.0 27.8 all-gather.12
  117.5 34.1 all-gather.14
  154.8 51.3 reduce-scatter.6
  227.5 92.7 reduce-scatter.4
  324.2 115.9 reduce-scatter.8
  444.2 115.9 reduce-scatter.10
  563.5 122.3 all-reduce.6
where the time goes:
time: 700 us; the launch traced here: 699 us
  waiting for transfers between devices  438 us (63%)
  matrix products  103 us (15%)
  local copies, waits for them, and re-layouts  50.6 us (7%)
  blocking collectives  49.2 us (7%)
  other arithmetic  35.8 us (5%)
  between operations  15 us (2%)
    reduce_scatter x1, waiting for transfers between devices, shards(): lax.psum_scatter(grad_up, 'sq', scatter_dimension=0, tiled=True)  118 us
    reduce_scatter x1, waiting for transfers between devices, shards(): lax.psum_scatter(grad_down, 'sq', scatter_dimension=0, tiled=True)  117 us
    psum x1, waiting for transfers between devices, shards(): lax.psum(shares_sq[1].astype(jnp.bfloat16), 'dp').astype(jnp.float32)  81.7 us
    reduce_scatter x1, waiting for transfers between devices, shards(): lax.psum_scatter(grad_qkv, 'sq', scatter_dimension=0, tiled=True)  67.5 us
    dot_general x4, matrix products, contract_rows(): lax.dot_general(left, right, (((0,), (0,)), ((), ())), preferred_element_...  31.4 us
    all_gather x1, waiting for transfers between devices, shards(): lax.all_gather(value_rows, 'sq', axis=1, tiled=True)  26.5 us
    all_gather x1, waiting for transfers between devices, shards(): lax.all_gather(key_rows, 'sq', axis=1, tiled=True)  26 us
    dot_general x4, matrix products, times_transpose(): lax.dot_general(left, right, (((1,), (1,)), ((), ())), preferred_element_...  18.2 us
  transfers between devices with their start and end apart: 9, of which 6 were waited for; matrix products, arithmetic and copies ran while one was open for 24% of the time, Pallas kernels for 0%

commit v1 on v0

--- a/solution.py
+++ b/solution.py
@@ -8,6 +8,27 @@
 EPSILON = 1e-05
 NEG_FILL = -1000000000.0
 START_MAX = -1e30
+
+
+def ring_gather(x, axis, dim):
+    count, place, span = (lax.axis_size(axis), lax.axis_index(axis), x.shape[dim])
+    right = [(i, (i + 1) % count) for i in range(count)]
+    left = [(i, (i - 1) % count) for i in range(count)]
+    filled = jnp.zeros((*x.shape[:dim], count * span, *x.shape[dim + 1 :]), x.dtype)
+    filled = lax.dynamic_update_slice_in_dim(filled, x, place * span, axis=dim)
+    from_left = from_right = x
+    halfway = count // 2
+    for step in range(1, halfway + 1):
+        from_left = lax.ppermute(from_left, axis, right)
+        filled = lax.dynamic_update_slice_in_dim(
+            filled, from_left, (place - step) % count * span, axis=dim
+        )
+        if step < count - halfway:
+            from_right = lax.ppermute(from_right, axis, left)
+            filled = lax.dynamic_update_slice_in_dim(
+                filled, from_right, (place + step) % count * span, axis=dim
+            )
+    return filled
 
 
 def norm_scaled(values, gain):
@@ -127,10 +148,7 @@
     )
     final_max, final_sum, accum = over_blocks(
         start_state,
-        (
-            lax.all_gather(key_rows, "sq", axis=1, tiled=True),
-            lax.all_gather(value_rows, "sq", axis=1, tiled=True),
-        ),
+        (lax.all_gather(key_rows, "sq", axis=1, tiled=True), ring_gather(value_rows, "sq", 1)),
         jnp.int32(0),
         forward_step,
         512,

time: 700 us -> 692 us (0.989)
  waiting for transfers between devices: 438 us -> 400 us
  local copies, waits for them, and re-layouts: 50.6 us -> 63.8 us
  starting transfers between devices: 0.63 us -> 9.32 us
    all_gather x1, waiting for transfers between devices: 26.5 us -> 0.01 us  [shards(): lax.all_gather(value_rows, 'sq', axis=1, tiled=True)]
    all_gather x1, waiting for transfers between devices: 26 us -> 0.01 us  [shards(): lax.all_gather(key_rows, 'sq', axis=1, tiled=True)]
    ppermute x0 -> x7, waiting for transfers between devices: none -> 15 us  [the longest x4 8.78 us: ring_gather(): from_left = lax.ppermute(from_left, axis, right)]
    ppermute x0 -> x7, starting transfers between devices: none -> 8.74 us  [the longest x3 7.74 us: ring_gather(): from_right = lax.ppermute(from_right, axis, left)]
    dynamic_update_slice x0 -> x8, local copies, waits for them, and re-layouts: none -> 8.6 us  [the longest x4 4.78 us: ring_gather(): lax.dynamic_update_slice_in_dim(filled, from_left, (place - step) % count...]
    unnamed x94 -> x92, local copies, waits for them, and re-layouts: 17.1 us -> 17 us
  transfers between devices with their start and end apart: 9 -> 16, of which waited for: 6 -> 8; matrix products, arithmetic and copies ran while one was open for 24% -> 26% of each run, Pallas kernels for 0% -> 0%
where the time goes in v1:
time: 692 us; the launch traced here: 685 us
  waiting for transfers between devices  400 us (58%)
  matrix products  103 us (15%)
  local copies, waits for them, and re-layouts  63.8 us (9%)
  blocking collectives  49.6 us (7%)
  other arithmetic  37.3 us (5%)
  between operations  15.3 us (2%)
  starting transfers between devices  9.32 us (1%)
    reduce_scatter x1, waiting for transfers between devices, shards(): lax.psum_scatter(grad_up, 'sq', scatter_dimension=0, tiled=True)  118 us
    reduce_scatter x1, waiting for transfers between devices, shards(): lax.psum_scatter(grad_down, 'sq', scatter_dimension=0, tiled=True)  117 us
    psum x1, waiting for transfers between devices, shards(): lax.psum(shares_sq[1].astype(jnp.bfloat16), 'dp').astype(jnp.float32)  81.7 us
    reduce_scatter x1, waiting for transfers between devices, shards(): lax.psum_scatter(grad_qkv, 'sq', scatter_dimension=0, tiled=True)  67.4 us
    dot_general x4, matrix products, contract_rows(): lax.dot_general(left, right, (((0,), (0,)), ((), ())), preferred_element_...  31.5 us
    dot_general x4, matrix products, times_transpose(): lax.dot_general(left, right, (((1,), (1,)), ((), ())), preferred_element_...  18.2 us
    unnamed x92, local copies, waits for them, and re-layouts  17 us
    all_gather x1, blocking collectives, shards(): lax.all_gather(delta_rows.astype(jnp.bfloat16), 'sq', axis=1, tiled=True)  15.2 us
  transfers between devices with their start and end apart: 16, of which 8 were waited for; matrix products, arithmetic and copies ran while one was open for 26% of the time, Pallas kernels for 0%

profile of v1, /device:TPU:0, one launch (start us, length us, event | category | flops | bytes accessed | tf_op | source)
XLA Modules:
  0.0 684.9 jit_solution(7976593075149619330)
XLA Ops:
  18.3 4.2 collective-permute-done
  41.4 6.2 collective-permute-done.5
  59.6 14.3 %while.45 = (s32[]{:T(128)}, f32[1,16,128]{2,1,0:T(8,128)S(1)}, f32[1,16,128]{2,1,0:T(8,128)S(1)}, f32[1,16,128,64]{2,3,1,0:T(8,128)S(1)}, s32[2]{0:T(128)S(1)},...) while((s32[]{:T(128)}, f32[1,16,128]{2,1,0:T(8,128)S(1)}, ...), condition=%wide.region_9.10_spmd, body=%wide.region_3.9_spmd.sunk | while | flops 282544640 | bytes 20628860 | solution.py:73
  63.4 6.1 conditional.8
  79.3 4.8 fusion.92
  84.1 7.7 %fusion.60 = bf16[128,4096]{1,0:T(8,128)(2,1)S(1)} fusion(f32[128,4096]{1,0:T(8,128)S(1)} %fusion.92, bf16[4096,1024]{1,0:T(8,128)(2,1)} %param.27, bf16[1,128,1024]{2,1,0:T(8,128)(2,1)S(1)} %copy-done.19), kind=kOutput, calls=%fused_computation.80 | convolution fusion | flops 1084227584 | bytes 11796480 | tf_op jit(solution)/shard_map/dot_general | solution.py:83
  105.0 4.0 copy.72
  110.6 15.2 %all_gather.24 = bf16[1,1024,16]{1,2,0:T(8,128)(2,1)S(1)} all-gather(bf16[1,128,16]{1,2,0:T(8,128)(2,1)S(1)} %bitcast_convert_fusion), channel_id=1, replica_groups=mesh['dp'=4,'sq'=8] {'sq'}, dimensions={1}, use_global_device_ids=true | all-gather | bytes 36864 | tf_op jit(solution)/shard_map/all_gather | solution.py:271
  126.4 8.1 %all_gather.22 = bf16[1,1024,16]{1,2,0:T(8,128)(2,1)S(1)} all-gather(bf16[1,128,16]{1,2,0:T(8,128)(2,1)S(1)} %get-tuple-element.1073), channel_id=1, replica_groups=mesh['dp'=4,'sq'=8] {'sq'}, dimensions={1}, use_global_device_ids=true | all-gather | bytes 36864 | tf_op jit(solution)/shard_map/all_gather | solution.py:268
  134.5 4.1 copy.69
  140.7 20.1 %while.46 = (s32[]{:T(128)}, f32[1,16,128,64]{2,3,1,0:T(8,128)}, s32[2]{0:T(128)}, s32[128]{0:T(128)}, s32[1,8]{1,0:T(1,128)}, /*index=5*/s32[1,128]{1,0:T(1,128...) while((s32[]{:T(128)}, f32[1,16,128,64]{2,3,1,0:T(8,128)}, ...), condition=%wide.region_17.18_spmd, body=%wide.region_13.17_spmd.sunk | while | flops 409285120 | bytes 17499484 | solution.py:73
  145.0 11.5 %conditional.9 = (f32[1,16,128,64]{2,3,1,0:T(8,128)}) conditional(s32[]{:T(128)} %convert_element_type.291, f32[1,16,128,64]{2,3,1,0:T(8,128)} %get-tuple-element.1438, (s32[]{:T(128)}, s32[512]{0:T(512)S(1)}, s32[128]{0:T(128)}, s32[1,512,8]{1,2,0:T(8,128)S(1)}, s32[1,128]{1,0:T(1,128)}, /*index=5*/bf16[2,1,512,1024]{2,3,1,0:T(8,128)(2,1)}, ...), branch_computations={%region_14.14_spmd, %region_15.16_spmd} | conditional | flops 409276416 | bytes 17476628 | solution.py:210
  150.9 5.6 fusion.23
  162.6 4.0 copy.74
  167.5 37.0 %while.47 = (s32[]{:T(128)}, f32[1,16,128,64]{2,3,1,0:T(8,128)S(1)}, f32[1,16,128,64]{2,3,1,0:T(8,128)}, s32[2]{0:T(128)S(1)}, s32[]{:T(128)}, /*index=5*/s32[1,...) while((s32[]{:T(128)}, ...), condition=%wide.region_22.23_spmd.clone.clone, body=%wide.region_18.22_spmd.clone.clone.sunk | while | flops 547828352 | bytes 28265440 | solution.py:73
  169.5 16.5 %conditional.10 = ((f32[1,16,128,64]{2,3,1,0:T(8,128)S(1)}, f32[1,16,128,64]{2,3,1,0:T(8,128)})) conditional(s32[]{:T(128)} %convert_element_type.293, (f32[1,16,128,64]{2,3,1,0:T(8,128)S(1)}, f32[1,16,128,64]{2,3,1,0:T(8,128)}) %tuple.151, (s32[]{:T(128)}, s32[]{:T(128)}, s32[512]{0:T(512)S(1)}, s32[1,128]{1,0:T(1,128)}, ...), branch_computations={%region_19.19_spmd, %region_20.21_spmd} | conditional | flops 547819648 | bytes 28242020 | solution.py:261
  175.6 6.2 fusion.42
  181.8 4.2 fusion.43
  187.9 16.6 %conditional.10 = ((f32[1,16,128,64]{2,3,1,0:T(8,128)S(1)}, f32[1,16,128,64]{2,3,1,0:T(8,128)})) conditional(s32[]{:T(128)} %convert_element_type.293, (f32[1,16,128,64]{2,3,1,0:T(8,128)S(1)}, f32[1,16,128,64]{2,3,1,0:T(8,128)}) %tuple.151, (s32[]{:T(128)}, s32[]{:T(128)}, s32[512]{0:T(512)S(1)}, s32[1,128]{1,0:T(1,128)}, ...), branch_computations={%region_19.19_spmd, %region_20.21_spmd} | conditional | flops 547819648 | bytes 28242020 | solution.py:261
  194.1 6.2 fusion.42
  200.3 4.2 fusion.43
  205.7 7.5 %fusion.72 = f32[1024,3072]{1,0:T(8,128)} fusion(bf16[128,1024]{0,1:T(8,128)(2,1)S(1)} %bitcast.232, bf16[128,1024]{0,1:T(8,128)(2,1)S(1)} %bitcast.234, bf16[128,1024]{0,1:T(8,128)(2,1)} %bitcast.230, bf16[1,128,1024]{2,1,0:T(8,128)(2,1)S(1)} %copy-done.4, f32[1024]{0:T(1024)S(1)} %copy-done.31, f32[128]{0:T(128)S(1)} %copy-done.37), kind=kOutput, calls=%fused_computation.111 | convolution fusion | flops 808189952 | bytes 13636096 | tf_op jit(solution)/shard_map/dot_general | solution.py:77
  214.4 11.3 %fusion.91 = f32[1024,4096]{1,0:T(8,128)} fusion(bf16[128,4096]{1,0:T(8,128)(2,1)S(1)} %copy-done.9, f32[128,1024]{1,0:T(8,128)S(1)} %get-tuple-element.1090, f32[1024]{0:T(1024)S(1)} %copy-done.30, f32[128]{0:T(128)S(1)} %copy-done.34), kind=kOutput, calls=%fused_computation.148 | convolution fusion | flops 1074135040 | bytes 18354688 | tf_op jit(solution)/shard_map/dot_general | solution.py:77
  227.9 8.8 %fusion.74 = f32[4096,1024]{1,0:T(8,128)} fusion(bf16[1,128,1024]{2,1,0:T(8,128)(2,1)S(1)} %copy-done.20, f32[128,4096]{1,0:T(8,128)S(1)} %copy-done.3), kind=kOutput, calls=%fused_computation.113 | convolution fusion | flops 1078460416 | bytes 19136512 | tf_op jit(solution)/shard_map/dot_general | solution.py:77
  238.6 67.4 %reduce-scatter.5.cloned.1.call-done = f32[128,3072]{1,0:T(8,128)} async-done(((f32[1024,3072]{1,0:T(8,128)}), f32[128,3072]{1,0:T(8,128)}) %reduce-scatter.5.cloned.1.call-update) | async-done | bytes 1572880 | tf_op jit(solution)/shard_map/reduce_scatter | solution.py:294
  308.4 117.6 %reduce-scatter.9.cloned.1.call-done = f32[128,4096]{1,0:T(8,128)} async-done(((f32[1024,4096]{1,0:T(8,128)}), f32[128,4096]{1,0:T(8,128)}) %reduce-scatter.9.cloned.1.call-update) | async-done | bytes 2097168 | tf_op jit(solution)/shard_map/reduce_scatter | solution.py:297
  428.7 117.3 %reduce-scatter.11.cloned.1.call-done = f32[512,1024]{1,0:T(8,128)} async-done(((f32[4096,1024]{1,0:T(8,128)}), f32[512,1024]{1,0:T(8,128)}) %reduce-scatter.11.cloned.1.call-update) | async-done | bytes 2097168 | tf_op jit(solution)/shard_map/reduce_scatter | solution.py:298
  550.6 5.7 fusion.62
  556.4 5.2 fusion.66
  561.5 13.8 %all-reduce.2 = (bf16[1024]{0:T(1024)(128)(2,1)S(1)}, bf16[1024]{0:T(1024)(128)(2,1)S(1)}) all-reduce(f32[1024]{0:T(1024)S(1)} %get-tuple-element.989, f32[1024]{0:T(1024)S(1)} %copy-done.35), channel_id=6, replica_groups=mesh['dp'=4,'sq'=8] {'sq'}, use_global_device_ids=true, to_apply=%region_25.26.clone | all-reduce | flops 2048 | bytes 12288
  575.5 12.4 %all-reduce.3 = (bf16[128]{0:T(256)(128)(2,1)S(1)}, bf16[128]{0:T(256)(128)(2,1)S(1)}) all-reduce(bf16[128]{0:T(256)(128)(2,1)S(1)} %dynamic-slice.7, bf16[128]{0:T(256)(128)(2,1)S(1)} %dynamic-slice.6), channel_id=1, replica_groups=mesh['dp'=4,'sq'=8] {'dp'}, use_global_device_ids=true, to_apply=%region_26.27 | all-reduce | flops 256 | bytes 1024 | tf_op jit(solution)/shard_map/psum | solution.py:301
  590.0 81.7 %all-reduce.7.cloned.1.call-done = (bf16[128,3072]{1,0:T(8,128)(2,1)}, bf16[128,1024]{1,0:T(8,128)(2,1)}, bf16[128,4096]{1,0:T(8,128)(2,1)}, bf16[512,1024]{1,0:T(8,128)(2,1)}) async-done(((bf16[128,3072]{1,0:T(8,128)(2,1)}, bf16[128,1024]{1,0:T(8,128)(2,1)}, bf16[128,4096]{1,0:T(8,128)(2,1)}, bf16[512,1024]{1,0:T(8,128)(2,1)}), (bf16[128,3072]{1,0:T(8,128)(2,1)}, bf16[128,1024]{1,0:T(8,128)(2,1)}, ...) | async-done | bytes 3145744 | tf_op jit(solution)/shard_map/psum | solution.py:302
  (256 shorter events, 129.1 us)
Async XLA Ops:
  7.2 70.4 %copy-start = (bf16[1024,1024]{1,0:T(8,128)(2,1)S(1)}, bf16[1024,1024]{1,0:T(8,128)(2,1)}, u32[]{:S(2)}) copy-start(bf16[1024,1024]{1,0:T(8,128)(2,1)} %param.24) | copy-start | bytes 6291460
  7.2 48.4 %all-gather.9.cloned.1.call-start = ((), (), s32[]{:S(2)}) async-start(), calls=%async_computation.8 | async-start | bytes 2359296 | tf_op jit(solution)/shard_map/all_gather | solution.py:151
  13.9 11.3 %copy-start.41 = (s32[1,8]{1,0:T(1,128)S(1)}, s32[1,8]{1,0:T(1,128)}, u32[]{:S(2)}) copy-start(s32[1,8]{1,0:T(1,128)} %param.28) | copy-start | bytes 100
  13.9 16.0 %copy-start.11 = (bf16[128,1024]{1,0:T(8,128)(2,1)S(1)}, bf16[128,1024]{1,0:T(8,128)(2,1)}, u32[]{:S(2)}) copy-start(bf16[128,1024]{1,0:T(8,128)(2,1)} %get-tuple-element.1087) | copy-start | bytes 786436
  13.9 91.0 %all-gather.13.cloned.1.call-start = ((), (), s32[]{:S(2)}) async-start(), calls=%async_computation.10 | async-start | bytes 2359296 | tf_op jit(solution)/shard_map/all_gather | solution.py:266
  14.7 119.8 %all-gather.11.cloned.1.call-start = ((), (), s32[]{:S(2)}) async-start(), calls=%async_computation.9 | async-start | bytes 2359296 | tf_op jit(solution)/shard_map/all_gather | solution.py:217
  14.7 7.7 %collective-permute-start = (bf16[1,128,1024]{2,1,0:T(8,128)(2,1)S(1)}, bf16[1,128,1024]{2,1,0:T(8,128)(2,1)}, u32[]{:S(2)}, u32[]{:S(2)}) collective-permute-start(bf16[1,128,1024]{2,1,0:T(8,128)(2,1)S(1)} %get-tuple-element.1086), channel_id=1, source_target_pairs={{0,1},{1,2},{2,3},{3,4},{4,5},{5,6},{6,7},{7,0},{8,9},{9,10},{10,1... | collective-permute-start | bytes 786440 | tf_op jit(solution)/shard_map/ppermute | solution.py:22
  15.2 11.3 %collective-permute-start.1 = (bf16[1,128,1024]{2,1,0:T(8,128)(2,1)S(1)}, bf16[1,128,1024]{2,1,0:T(8,128)(2,1)}, u32[]{:S(2)}, u32[]{:S(2)}) collective-permute-start(bf16[1,128,1024]{2,1,0:T(8,128)(2,1)S(1)} %get-tuple-element.1086), channel_id=1, source_target_pairs={{0,7},{1,0},{2,1},{3,2},{4,3},{5,4},{6,5},{7,6},{8,15},{9,8},{10,9... | collective-permute-start | bytes 786440 | tf_op jit(solution)/shard_map/ppermute | solution.py:27
  18.2 144.4 %all-gather.15.cloned.1.call-start = ((), (), s32[]{:S(2)}) async-start(), calls=%async_computation.11 | async-start | bytes 2359296 | tf_op jit(solution)/shard_map/all_gather | solution.py:267
  22.4 9.8 %collective-permute-start.2 = (bf16[1,128,1024]{2,1,0:T(8,128)(2,1)}, bf16[1,128,1024]{2,1,0:T(8,128)(2,1)}, u32[]{:S(2)}, u32[]{:S(2)}) collective-permute-start(bf16[1,128,1024]{2,1,0:T(8,128)(2,1)} %collective-permute-done), channel_id=1, source_target_pairs={{0,1},{1,2},{2,3},{3,4},{4,5},{5,6},{6,7},{7,0},{8,9},{9,10},{10,1... | collective-permute-start | bytes 786440 | tf_op jit(solution)/shard_map/ppermute | solution.py:22
  26.5 9.1 %collective-permute-start.3 = (bf16[1,128,1024]{2,1,0:T(8,128)(2,1)}, bf16[1,128,1024]{2,1,0:T(8,128)(2,1)S(1)}, u32[]{:S(2)}, u32[]{:S(2)}) collective-permute-start(bf16[1,128,1024]{2,1,0:T(8,128)(2,1)} %collective-permute-done.1), channel_id=1, source_target_pairs={{0,7},{1,0},{2,1},{3,2},{4,3},{5,4},{6,5},{7,6},{8,15},{9,8},{10,9... | collective-permute-start | bytes 786440 | tf_op jit(solution)/shard_map/ppermute | solution.py:27
  32.3 7.7 %collective-permute-start.4 = (bf16[1,128,1024]{2,1,0:T(8,128)(2,1)}, bf16[1,128,1024]{2,1,0:T(8,128)(2,1)S(1)}, u32[]{:S(2)}, u32[]{:S(2)}) collective-permute-start(bf16[1,128,1024]{2,1,0:T(8,128)(2,1)} %collective-permute-done.2), channel_id=1, source_target_pairs={{0,1},{1,2},{2,3},{3,4},{4,5},{5,6},{6,7},{7,0},{8,9},{9,10},{10,1... | collective-permute-start | bytes 786440 | tf_op jit(solution)/shard_map/ppermute | solution.py:22
  35.6 12.0 %collective-permute-start.5 = (bf16[1,128,1024]{2,1,0:T(8,128)(2,1)S(1)}, bf16[1,128,1024]{2,1,0:T(8,128)(2,1)S(1)}, u32[]{:S(2)}, u32[]{:S(2)}) collective-permute-start(bf16[1,128,1024]{2,1,0:T(8,128)(2,1)S(1)} %collective-permute-done.3), channel_id=1, source_target_pairs={{0,7},{1,0},{2,1},{3,2},{4,3},{5,4},{6,5},{7,6},{8,15},{9,8},{10,9... | collective-permute-start | bytes 786440 | tf_op jit(solution)/shard_map/ppermute | solution.py:27
  39.9 11.0 %collective-permute-start.6 = (bf16[1,128,1024]{2,1,0:T(8,128)(2,1)S(1)}, bf16[1,128,1024]{2,1,0:T(8,128)(2,1)S(1)}, u32[]{:S(2)}, u32[]{:S(2)}) collective-permute-start(bf16[1,128,1024]{2,1,0:T(8,128)(2,1)S(1)} %collective-permute-done.4), channel_id=1, source_target_pairs={{0,1},{1,2},{2,3},{3,4},{4,5},{5,6},{6,7},{7,0},{8,9},{9,10},{10,1... | collective-permute-start | bytes 786440 | tf_op jit(solution)/shard_map/ppermute | solution.py:22
  79.2 16.2 %copy-start.33 = (f32[128]{0:T(128)}, f32[128]{0:T(128)S(1)}, u32[]{:S(2)}) copy-start(f32[128]{0:T(128)S(1)} %fusion.88) | copy-start | bytes 1540
  79.2 12.7 %slice-start = ((s8[8388608]{0:T(1024)(128)(4,1)}), s8[4194304]{0:T(1024)(128)(4,1)S(1)}, s32[]{:S(2)}) async-start(s8[8388608]{0:T(1024)(128)(4,1)} %bitcast.213), calls=%async_computation.13 | async-start | bytes 8388608
  84.1 7.8 %copy-start.2 = (f32[128,4096]{1,0:T(8,128)}, f32[128,4096]{1,0:T(8,128)S(1)}, u32[]{:S(2)}) copy-start(f32[128,4096]{1,0:T(8,128)S(1)} %fusion.92) | copy-start | bytes 6291460
  84.1 7.8 %slice-start.1 = ((s8[8388608]{0:T(1024)(128)(4,1)}), s8[4194304]{0:T(1024)(128)(4,1)S(1)}, s32[]{:S(2)}) async-start(s8[8388608]{0:T(1024)(128)(4,1)} %bitcast.213), calls=%async_computation.14 | async-start | bytes 8388608
  98.3 138.6 %reduce-scatter.7.cloned.1.call-start = ((), (), s32[]{:S(2)}) async-start(), calls=%async_computation.5 | async-start | bytes 4718592 | tf_op jit(solution)/shard_map/reduce_scatter | solution.py:295
  102.2 203.8 %reduce-scatter.5.cloned.1.call-start = ((), (), s32[]{:S(2)}) async-start(), calls=%async_computation.4 | async-start | bytes 14155776 | tf_op jit(solution)/shard_map/reduce_scatter | solution.py:294
  167.5 38.2 %copy-start.31 = (f32[1024]{0:T(1024)S(1)}, f32[1024]{0:T(1024)}, u32[]{:S(2)}) copy-start(f32[1024]{0:T(1024)} %param.22) | copy-start | bytes 12292
  167.5 38.2 %copy-start.37 = (f32[128]{0:T(128)S(1)}, f32[128]{0:T(128)}, u32[]{:S(2)}) copy-start(f32[128]{0:T(128)} %copy-done.36) | copy-start | bytes 1540
  205.6 7.6 %copy-start.24 = (bf16[1,16,128,64]{2,3,1,0:T(8,128)(2,1)}, bf16[1,16,128,64]{2,3,1,0:T(8,128)(2,1)S(1)}, u32[]{:S(2)}) copy-start(bf16[1,16,128,64]{2,3,1,0:T(8,128)(2,1)S(1)} %convert.20) | copy-start | bytes 786436
  205.7 7.5 %copy-start.26 = (bf16[1,16,128,64]{2,3,1,0:T(8,128)(2,1)}, bf16[1,16,128,64]{2,3,1,0:T(8,128)(2,1)S(1)}, u32[]{:S(2)}) copy-start(bf16[1,16,128,64]{2,3,1,0:T(8,128)(2,1)S(1)} %multiply_convert_fusion.2) | copy-start | bytes 786436
  213.2 212.7 %reduce-scatter.9.cloned.1.call-start = ((), (), s32[]{:S(2)}) async-start(), calls=%async_computation.6 | async-start | bytes 18874368 | tf_op jit(solution)/shard_map/reduce_scatter | solution.py:297
  225.8 320.2 %reduce-scatter.11.cloned.1.call-start = ((), (), s32[]{:S(2)}) async-start(), calls=%async_computation.7 | async-start | bytes 18874368 | tf_op jit(solution)/shard_map/reduce_scatter | solution.py:298
  236.8 434.9 %all-reduce.7.cloned.1.call-start = ((), (), s32[]{:S(2)}) async-start(), calls=%async_computation.12 | async-start | bytes 6291456 | tf_op jit(solution)/shard_map/psum | solution.py:302
  550.6 5.7 copy-start.23
  550.6 5.7 copy-start.25
  550.6 5.7 copy-start.27
  556.3 32.7 %copy-start.40 = (f32[128]{0:T(128)S(1)}, f32[128]{0:T(128)}, u32[]{:S(2)}) copy-start(f32[128]{0:T(128)} %copy-done.39) | copy-start | bytes 1540
  556.4 32.7 %copy-start.6 = (f32[128,1024]{1,0:T(8,128)S(1)}, f32[128,1024]{1,0:T(8,128)}, u32[]{:S(2)}) copy-start(f32[128,1024]{1,0:T(8,128)} %copy-done.5) | copy-start | bytes 1572868
  (31 other events, 76.6 us)
Sparse Core Ops, SparseCore 0:
  14.1 36.0 all-gather.8
  52.0 27.9 all-gather.12
  82.5 27.9 all-gather.10
  112.2 28.0 all-gather.14
  143.4 51.3 reduce-scatter.6
  213.4 92.6 reduce-scatter.4
  310.0 115.9 reduce-scatter.8
  430.0 115.9 reduce-scatter.10
  549.3 122.2 all-reduce.6
